TPU v7x, 1024 devices: a whole 8x8x8 slice. The times are simulated.
1024 devices in a mesh: expert: 64 (over y, z_hi, core), tensor: 16 (over z_lo, x).
Axes of the slice: x: 8, y: 8, z: 8 (z_hi: 4, z_lo: 2; z = z_hi * 2 + z_lo), core: 2. Of those that a mesh axis runs over, the one named last changes fastest.
Arguments:
- tokens: bfloat16 [4096, 4096], P('expert', 'tensor'), may hold values from -6 to 6
- expert_ids: int32 [4096, 8], P('expert'), may hold values from 0 to 63, all different within a row; in each aligned block of 64 rows (0 to 63, 64 to 127, ...) at most 12 rows name the same one
- gate_weights: float32 [4096, 8], P('expert'), may hold values from 0.1 to 1
- w_gate: bfloat16 [64, 4096, 1536], P('expert', None, 'tensor'), may hold values from -0.09375 to 0.09375
- w_up: bfloat16 [64, 4096, 1536], P('expert', None, 'tensor'), may hold values from -0.09375 to 0.09375
- w_down: bfloat16 [64, 1536, 4096], P('expert', 'tensor'), may hold values from -0.15625 to 0.15625
Outputs:
- mixed: bfloat16 [4096, 4096], P('expert', 'tensor')
Inputs may be any that keep to these rules, and one draw needn't show every extreme that they name: `expert_ids`: each row names 8 different experts. Within each aligned block of 64 rows no expert is named by more than 12 rows, and in every draw some expert is named by exactly 12 rows of some block.
All inputs are finite; a program needn't handle non-finite values.
Results may differ from a plain program's by a relative error of at most 0.02.
Values may be sent and summed in bfloat16 or wider, within the bound.
A program may use at most 64 MiB of HBM per device.

v0:
```python
import jax
import jax.numpy as jnp
from jax import lax
from jax.sharding import PartitionSpec as P


def laid_out(blocks, dim):
    dims = list(blocks.shape[1:])
    dims[dim] *= blocks.shape[0]
    return jnp.moveaxis(blocks, 0, dim).reshape(dims)


def copy_for_each(shard, axis):
    copies = jnp.broadcast_to(shard, (lax.axis_size(axis), *shard.shape))
    return lax.all_to_all(copies, axis, split_axis=0, concat_axis=0, tiled=True)


def gathered_copies(shard, axis, dim):
    return laid_out(copy_for_each(shard, axis), dim)


def local(tokens, expert_ids, gate_weights, w_gate, w_up, w_down):
    experts = lax.axis_size("expert")
    tok_rows, top_count = expert_ids.shape
    capacity = min(tok_rows, 3 * tok_rows * top_count // (2 * experts))
    slots_all = experts * capacity
    flat_ids = expert_ids.reshape(-1)
    onehot = (flat_ids[:, None] == jnp.arange(experts, dtype=jnp.int32)[None, :]).astype(jnp.int32)
    slot_rank = jnp.sum((jnp.cumsum(onehot, axis=0) - onehot) * onehot, axis=1)
    places = (flat_ids * capacity + slot_rank).reshape(tok_rows, top_count)
    slot_range = jnp.arange(slots_all, dtype=jnp.int32)[None, :]
    selector = jnp.zeros((tok_rows, slots_all), jnp.float32)
    combine_weights = jnp.zeros((tok_rows, slots_all), jnp.float32)
    for choice_index in range(top_count):
        hit = places[:, choice_index][:, None] == slot_range
        selector = selector + hit.astype(jnp.float32)
        combine_weights = combine_weights + jnp.where(
            hit, gate_weights[:, choice_index][:, None], 0.0
        )
    selector = selector.astype(jnp.bfloat16)
    outgoing = lax.dot_general(
        selector, tokens, (((0,), (0,)), ((), ())), preferred_element_type=jnp.float32
    ).astype(jnp.bfloat16)
    arrived = lax.all_to_all(outgoing, "expert", split_axis=0, concat_axis=0, tiled=True)
    recv_rows = arrived.shape[0]
    hidden_units = w_gate.shape[2]
    paired = jnp.concatenate([w_gate[0], w_up[0]], axis=1)
    weight_block = paired
    gate_up = jnp.dot(
        lax.all_gather(arrived, "tensor", axis=1, tiled=True),
        weight_block,
        preferred_element_type=jnp.float32,
    )
    hidden = (jax.nn.silu(gate_up[:, :hidden_units]) * gate_up[:, hidden_units:]).astype(
        jnp.bfloat16
    )
    down_rows = w_down[0]
    columns = lax.all_to_all(down_rows, "tensor", split_axis=1, concat_axis=0, tiled=True)
    piece = gathered_copies(hidden, "tensor", 1)
    piece_width = piece.shape[1]
    blocks_per = piece_width // hidden_units
    weight_block = columns
    weight_block = weight_block.reshape(blocks_per, hidden_units, columns.shape[1])
    partial_value = jnp.einsum(
        "rbf,bfd->bdr",
        piece.reshape(recv_rows, blocks_per, hidden_units),
        weight_block,
        preferred_element_type=jnp.float32,
    )
    rounded = lax.optimization_barrier(partial_value.astype(jnp.bfloat16))
    summed = jnp.sum(rounded.astype(jnp.float32), axis=0)
    expert_out = summed.astype(jnp.bfloat16)
    returned = lax.all_to_all(expert_out, "expert", split_axis=1, concat_axis=1, tiled=True)
    mixed = lax.dot_general(
        combine_weights,
        returned.astype(jnp.float32),
        (((1,), (1,)), ((), ())),
        precision=lax.Precision.HIGHEST,
        preferred_element_type=jnp.float32,
    )
    return mixed.astype(jnp.bfloat16)


def solution(mesh):
    placed = (
        P("expert", "tensor"),
        P("expert", None),
        P("expert", None),
        P("expert", None, "tensor"),
        P("expert", None, "tensor"),
        P("expert", "tensor", None),
    )
    return jax.shard_map(
        local, mesh=mesh, in_specs=placed, out_specs=P("expert", "tensor"), check_vma=False
    )
```

profile of v0, /device:TPU:1, one launch (start us, length us, event | category | flops | bytes accessed | tf_op | source)
XLA Modules:
  0.0 276.5 jit_solution(1674021230450385179)
XLA Ops:
  6.5 0.0 copy-start
  6.5 0.0 copy-start.1
  6.5 0.0 all-gather.2.cloned.1.call-start
  6.5 0.8 copy.19
  7.4 0.1 eq.149
  7.5 0.1 eq.145
  7.6 1.2 reduce-window.6
  8.8 0.2 slice_reduce_fusion
  9.1 0.1 fusion.24
  9.2 0.1 reduce_sum.24
  9.3 0.1 copy.22
  9.3 0.7 multiply_add_fusion
  10.1 0.0 copy-done
  10.1 0.5 convolution_convert_fusion
  10.5 0.1 all_to_all.31
  10.6 42.9 %all_to_all.45 = bf16[64,12,256]{2,1,0:T(8,128)(2,1)S(1)} all-to-all(bf16[64,12,256]{2,1,0:T(8,128)(2,1)S(1)} %all_to_all.31), channel_id=1, replica_groups=mesh['expert'=64,'tensor'=16] {'expert'}, dimensions={0} | all-to-all | bytes 786432 | tf_op jit(solution)/shard_map/all_to_all | solution.py:44
  53.6 0.0 copy-start.3
  53.6 0.0 copy-start.4
  53.6 0.8 all_to_all.33
  54.4 0.0 all-gather.2.cloned.1.call-update
  54.4 0.0 copy-done.1
  54.4 0.2 copy.25
  54.6 1.1 copy.23
  55.7 8.4 %all-to-all-start.2 = ((bf16[96,16,256]{2,0,1:T(8,128)(2,1)}), bf16[96,16,256]{2,0,1:T(8,128)(2,1)S(1)}, u32[]{:S(2)}, u32[]{:S(2)}) async-start(bf16[96,16,256]{2,0,1:T(8,128)(2,1)} %copy.23), calls=%async_computation.2 | async-start | bytes 1572864 | tf_op jit(solution)/shard_map/all_to_all | solution.py:58
  64.2 102.7 %all-gather.2.cloned.1.call-done = bf16[768,4096]{1,0:T(8,128)(2,1)} async-done(((bf16[768,256]{1,0:T(8,128)(2,1)}), bf16[768,4096]{1,0:T(8,128)(2,1)}) %all-gather.2.cloned.1.call-update) | async-done | bytes 6291472 | tf_op jit(solution)/shard_map/all_gather | solution.py:50
  166.9 0.0 copy-done.3
  166.9 0.0 copy-done.4
  166.9 5.0 %fusion.1 = f32[768,192]{0,1:T(8,128)S(1)} fusion(bf16[768,4096]{1,0:T(8,128)(2,1)} %all-gather.2.cloned.1.call-done, bf16[4096,96]{0,1:T(8,128)(2,1)S(1)} %bitcast.73, bf16[4096,96]{0,1:T(8,128)(2,1)S(1)} %bitcast.74), kind=kOutput, calls=%fused_computation.2 | convolution fusion | flops 1211105280 | bytes 8454144 | tf_op jit(solution)/shard_map/dot_general | solution.py:49
  171.9 0.1 fusion.6
  172.0 0.0 all-to-all-done.2
  172.0 0.2 broadcast_in_dim.92
  172.2 50.4 %all_to_all.46 = bf16[16,768,96]{1,2,0:T(8,128)(2,1)S(1)} all-to-all(bf16[16,768,96]{1,2,0:T(8,128)(2,1)S(1)} %broadcast_in_dim.92), channel_id=1, replica_groups=mesh['expert'=64,'tensor'=16] {'tensor'}, dimensions={0} | all-to-all | bytes 4718592 | tf_op jit(solution)/shard_map/all_to_all | solution.py:15
  222.6 4.5 %convert_bitcast_fusion = bf16[16,256,768]{1,2,0:T(8,128)(2,1)} fusion(bf16[16,768,96]{1,2,0:T(8,128)(2,1)S(1)} %all_to_all.46, bf16[96,16,256]{2,0,1:T(8,128)(2,1)S(1)} %all-to-all-done.2), kind=kOutput, calls=%fused_computation | convolution fusion | flops 607125504 | bytes 9437184 | tf_op jit(solution)/shard_map/rbf,bfd->bdr/dot_general | solution.py:64
  227.1 0.0 copy-start.2
  227.1 3.9 %reduce_sum.25 = bf16[256,768]{0,1:T(8,128)(2,1)S(1)} reduce(bf16[16,256,768]{1,2,0:T(8,128)(2,1)} %convert_bitcast_fusion, bf16[]{:T(256)} %constant.14.clone.1), dimensions={0}, to_apply=%region_3.4 | reduce | flops 2949120 | bytes 6684674 | tf_op jit(solution)/shard_map/reduce_sum | solution.py:71
  231.0 0.9 all_to_all.38
  231.8 17.0 %all-to-all-start.3 = ((bf16[256,64,12]{0,2,1:T(8,128)(2,1)}), bf16[256,64,12]{0,2,1:T(8,128)(2,1)S(1)}, u32[]{:S(2)}, u32[]{:S(2)}) async-start(bf16[256,64,12]{0,2,1:T(8,128)(2,1)} %all_to_all.38), calls=%async_computation.3 | async-start | bytes 1048576 | tf_op jit(solution)/shard_map/all_to_all | solution.py:73
  248.8 0.0 copy-done.2
  248.8 19.6 %all-to-all-done.3 = bf16[256,64,12]{0,2,1:T(8,128)(2,1)S(1)} async-done(((bf16[256,64,12]{0,2,1:T(8,128)(2,1)}), bf16[256,64,12]{0,2,1:T(8,128)(2,1)S(1)}, u32[]{:S(2)}, u32[]{:S(2)}) %all-to-all-start.3) | async-done | bytes 393248 | tf_op jit(solution)/shard_map/all_to_all | solution.py:73
  268.4 0.1 all_to_all.40
  268.5 1.2 convolution_convert_fusion.1
  (5 shorter events, 0.1 us)
Async XLA Ops:
  6.5 3.5 %copy-start = (bf16[64,256]{1,0:T(8,128)(2,1)S(1)}, bf16[64,256]{1,0:T(8,128)(2,1)}, u32[]{:S(2)}) copy-start(bf16[64,256]{1,0:T(8,128)(2,1)} %param.6) | copy-start | bytes 98308
  6.5 47.9 %copy-start.1 = (bf16[1,96,4096]{2,1,0:T(8,128)(2,1)S(1)}, bf16[1,96,4096]{2,1,0:T(8,128)(2,1)}, u32[]{:S(2)}) copy-start(bf16[1,96,4096]{2,1,0:T(8,128)(2,1)} %param.11) | copy-start | bytes 2359300
  6.5 160.3 %all-gather.2.cloned.1.call-start = ((), (), s32[]{:S(2)}) async-start(), calls=%async_computation.4 | async-start | bytes 6684672 | tf_op jit(solution)/shard_map/all_gather | solution.py:50
  53.6 113.3 %copy-start.3 = (bf16[1,4096,96]{1,2,0:T(8,128)(2,1)S(1)}, bf16[1,4096,96]{1,2,0:T(8,128)(2,1)}, u32[]{:S(2)}) copy-start(bf16[1,4096,96]{1,2,0:T(8,128)(2,1)} %param.10) | copy-start | bytes 2359300
  53.6 113.3 %copy-start.4 = (bf16[1,4096,96]{1,2,0:T(8,128)(2,1)S(1)}, bf16[1,4096,96]{1,2,0:T(8,128)(2,1)}, u32[]{:S(2)}) copy-start(bf16[1,4096,96]{1,2,0:T(8,128)(2,1)} %param.9) | copy-start | bytes 2359300
  55.7 116.2 %all-to-all-start.2 = ((bf16[96,16,256]{2,0,1:T(8,128)(2,1)}), bf16[96,16,256]{2,0,1:T(8,128)(2,1)S(1)}, u32[]{:S(2)}, u32[]{:S(2)}) async-start(bf16[96,16,256]{2,0,1:T(8,128)(2,1)} %copy.23), calls=%async_computation.2 | async-start | bytes 1572864 | tf_op jit(solution)/shard_map/all_to_all | solution.py:58
  227.1 21.7 %copy-start.2 = (f32[64,8]{0,1:T(8,128)S(1)}, f32[64,8]{0,1:T(8,128)}, u32[]{:S(2)}) copy-start(f32[64,8]{0,1:T(8,128)} %param.8) | copy-start | bytes 6148
  231.8 36.6 %all-to-all-start.3 = ((bf16[256,64,12]{0,2,1:T(8,128)(2,1)}), bf16[256,64,12]{0,2,1:T(8,128)(2,1)S(1)}, u32[]{:S(2)}, u32[]{:S(2)}) async-start(bf16[256,64,12]{0,2,1:T(8,128)(2,1)} %all_to_all.38), calls=%async_computation.3 | async-start | bytes 1048576 | tf_op jit(solution)/shard_map/all_to_all | solution.py:73
Sparse Core Ops, SparseCore 0:
  54.5 112.2 all-gather.1
where the time goes:
time: 277 us
  waiting for transfers between devices  122 us (44%)
  blocking collectives  93.3 us (34%)
  starting transfers between devices  25.4 us (9%)
  between operations  13.5 us (5%)
  matrix products  11.1 us (4%)
  other arithmetic  6.02 us (2%)
  local copies, waits for them, and re-layouts  4.86 us (2%)
    all_gather x1, waiting for transfers between devices, local(): lax.all_gather(arrived, 'tensor', axis=1, tiled=True)  103 us
    all_to_all x1, blocking collectives, copy_for_each(): return lax.all_to_all(copies, axis, split_axis=0, concat_axis=0, tiled=True)  50.4 us
    all_to_all x1, blocking collectives, local(): lax.all_to_all(outgoing, 'expert', split_axis=0, concat_axis=0, tiled=True)  42.9 us
    all_to_all x1, waiting for transfers between devices, local(): lax.all_to_all(expert_out, 'expert', split_axis=1, concat_axis=1, tiled=T...  19.6 us
    all_to_all x1, starting transfers between devices, local(): lax.all_to_all(expert_out, 'expert', split_axis=1, concat_axis=1, tiled=T...  17 us
    all_to_all x1, starting transfers between devices, local(): lax.all_to_all(down_rows, 'tensor', split_axis=1, concat_axis=0, tiled=True)  8.4 us
  transfers between devices with their start and end apart: 3, of which 2 were waited for; matrix products, arithmetic and copies ran while one was open for 2% of the time, Pallas kernels for 0%

commit v1 on v0

v1 whole, which is shorter than its diff:
```python
import functools

import jax
import jax.numpy as jnp
from jax import lax
from jax.experimental import pallas as pl
from jax.experimental.pallas import tpu as pltpu
from jax.sharding import PartitionSpec as P

MESH = pl.DeviceIdType.MESH
BF16, F32, I32 = jnp.bfloat16, jnp.float32, jnp.int32
CAP = 12
PAD = 16
CHUNKS = 2


def nt(a, b):
    return lax.dot_general(a, b, (((1,), (1,)), ((), ())), preferred_element_type=F32)


def nn(a, b):
    return jnp.dot(a, b, preferred_element_type=F32)


def tn(a, b):
    return lax.dot_general(a, b, (((0,), (0,)), ((), ())), preferred_element_type=F32)


def iota(shape, dim):
    return lax.broadcasted_iota(I32, shape, dim)


def kernel(
    E, NX,
    tok_ref, ids_ref, gw_ref, wg_ref, wu_ref, wd_ref, out_ref,
    send_buf, recv_buf, xa, xb, w1, acc, hid, wdn, out_acc, ret_src, ret_buf, comb,
    sem_w, sem_disp, sem_w1, sem_wds, sem_wdr, sem_fwd, sem_xs, sem_xr, sem_hs, sem_hr, sem_ret,
):
    HALF = E // 2
    TOK, F = tok_ref.shape
    U = wg_ref.shape[0]
    ROWS = HALF * CAP
    RC = ROWS // CHUNKS
    me = lax.axis_index("expert")
    s = lax.axis_index("tensor")
    z, x = s // NX, s % NX
    right, left = (x + 1) % NX, (x + NX - 1) % NX
    other = 1 - z
    home = me % 2
    own = home == z

    barrier = pltpu.get_barrier_semaphore()

    def greet(i, _):
        for zz in range(2):
            @pl.when(jnp.logical_not(jnp.logical_and(2 * i + z == me, zz == z)))
            def _():
                pl.semaphore_signal(barrier, inc=1, device_id=(2 * i + z, zz * NX + x), device_id_type=MESH)
        return 0

    lax.fori_loop(0, HALF, greet, 0)

    def greet_x(d, _):
        pl.semaphore_signal(barrier, inc=1, device_id=(me, z * NX + (x + d) % NX), device_id_type=MESH)
        return 0

    lax.fori_loop(1, NX, greet_x, 0)
    pl.semaphore_signal(barrier, inc=1, device_id=(me, other * NX + x), device_id_type=MESH)

    def cols(zz, xx):
        return pl.ds(pl.multiple_of(zz * (NX * F) + xx * F, F), F)

    def units(xx, zz):
        return pl.ds(pl.multiple_of((xx * 2 + zz) * U, U), U)

    load_g = pltpu.make_async_copy(wg_ref, w1.at[z, 0:U], sem_w.at[0])
    load_u = pltpu.make_async_copy(wu_ref, w1.at[z, U:2 * U], sem_w.at[1])
    load_d = [
        pltpu.make_async_copy(wd_ref.at[:, cols(f, x)], wdn.at[f, units(x, z)], sem_w.at[2 + f])
        for f in range(2)
    ]
    for c in (load_g, load_u, *load_d):
        c.start()

    ids = ids_ref[...]
    expert = iota((E, TOK), 0)
    member = jnp.zeros((E, TOK), jnp.bool_)
    weight = jnp.zeros((E, TOK), F32)
    for k in range(ids.shape[0]):
        hit = ids[k:k + 1, :] == expert
        member = jnp.logical_or(member, hit)
        weight = weight + jnp.where(hit, gw_ref[k:k + 1, :], 0.0)
    before = (iota((TOK, TOK), 0) < iota((TOK, TOK), 1)).astype(BF16)
    rank = nn(member.astype(F32).astype(BF16), before).astype(I32)
    rank = jnp.where(member, rank, PAD)
    slot = iota((E, PAD, TOK), 1)
    chosen = slot == rank[:, None, :]
    select = jnp.where(chosen, 1.0, 0.0).reshape(E * PAD, TOK).astype(BF16)
    send_buf[...] = nn(select, tok_ref[...]).astype(BF16).reshape(E, PAD, F)
    weights = jnp.where(chosen, weight[:, None, :], 0.0).reshape(E * PAD, TOK)
    high = weights.astype(BF16)
    comb[0] = high
    comb[1] = (weights - high.astype(F32)).astype(BF16)

    @pl.when(own)
    def _():
        pl.semaphore_wait(barrier, NX + E - 1)

    @pl.when(jnp.logical_not(own))
    def _():
        pl.semaphore_wait(barrier, NX + E)

    def dispatch(e, _):
        here = jnp.logical_and(e == me, own)

        @pl.when(here)
        def _():
            pltpu.make_async_copy(send_buf.at[e], recv_buf.at[z, me // 2], sem_disp.at[1]).start()

        @pl.when(jnp.logical_not(here))
        def _():
            pltpu.make_async_remote_copy(
                src_ref=send_buf.at[e], dst_ref=recv_buf.at[z, me // 2],
                send_sem=sem_disp.at[0], recv_sem=sem_disp.at[1],
                device_id=(e, home * NX + x), device_id_type=MESH,
            ).start()
        return 0

    lax.fori_loop(0, E, dispatch, 0)

    pair = (me, other * NX + x)
    send_w1 = [
        pltpu.make_async_remote_copy(
            src_ref=src, dst_ref=w1.at[z, j * U:(j + 1) * U],
            send_sem=sem_w1.at[0, j], recv_sem=sem_w1.at[1, j], device_id=pair, device_id_type=MESH,
        )
        for j, src in enumerate((wg_ref, wu_ref))
    ]
    for c in send_w1:
        c.start()

    def down(d, f):
        to = (x + d) % NX
        return pltpu.make_async_remote_copy(
            src_ref=wd_ref.at[:, cols(f, to)], dst_ref=wdn.at[f, units(x, z)],
            send_sem=sem_wds.at[d, f], recv_sem=sem_wdr.at[d, f],
            device_id=(me, z * NX + to), device_id_type=MESH,
        )

    def down_start(d, _):
        for f in range(2):
            down(d, f).start()
        return 0

    lax.fori_loop(1, NX, down_start, 0)

    def relay(d, f):
        part = wdn.at[f, units((x - d + NX) % NX, z)]
        return pltpu.make_async_remote_copy(
            src_ref=part, dst_ref=part, send_sem=sem_fwd.at[0, d, f], recv_sem=sem_fwd.at[1, d, f],
            device_id=pair, device_id_type=MESH,
        )

    everything = pltpu.make_async_copy(send_buf, send_buf, sem_disp.at[1])
    everything.wait()
    row, col = iota((ROWS, HALF * PAD), 0), iota((ROWS, HALF * PAD), 1)
    place = (col >> 4) * CAP + (col & 15)
    pack = jnp.logical_and(row == place, (col & 15) < CAP)
    pack = jnp.where(pack, 1.0, 0.0).astype(BF16)
    xa[x] = nn(pack, recv_buf[0].reshape(HALF * PAD, F)).astype(BF16)
    xb[x] = nn(pack, recv_buf[1].reshape(HALF * PAD, F)).astype(BF16)

    def ring(k, c, way):
        buf, shard, to = ((xa, (x - k + NX) % NX, right), (xb, (x + k) % NX, left))[way]
        part = buf.at[shard, pl.ds(c * RC, RC)]
        return pltpu.make_async_remote_copy(
            src_ref=part, dst_ref=part, send_sem=sem_xs.at[k, c, way], recv_sem=sem_xr.at[k, c, way],
            device_id=(me, z * NX + to), device_id_type=MESH,
        )

    def multiply(zz, k):
        a, b = (x - k + NX) % NX, (x + k) % NX
        acc[zz] += nt(w1[zz, :, cols(0, a)], xa[a]) + nt(w1[zz, :, cols(1, b)], xb[b])

    for c in range(CHUNKS):
        for way in range(2):
            ring(0, c, way).start()
    for c in (load_g, load_u, *load_d):
        c.wait()
    acc[...] = jnp.zeros_like(acc)
    multiply(z, 0)
    for f in range(2):
        relay(0, f).start()

    def ring_step(k, _):
        for c in range(CHUNKS):
            for way in range(2):
                ring(k - 1, c, way).wait_recv()

                @pl.when(k < NX - 1)
                def _():
                    ring(k, c, way).start()
        multiply(z, k)
        for f in range(2):
            down(k, f).wait_recv()
            relay(k, f).start()
        return 0

    lax.fori_loop(1, NX, ring_step, 0)

    for c in send_w1:
        c.wait_recv()

    def rest(k, _):
        multiply(other, k)
        return 0

    lax.fori_loop(0, NX, rest, 0)

    for zz in range(2):
        g, u = acc[zz, 0:U, :], acc[zz, U:2 * U, :]
        hid[x, zz * U:(zz + 1) * U, :] = (g / (1.0 + jnp.exp(-g)) * u).astype(BF16)

    def hring(k, way):
        shard, to = (((x - k + NX) % NX, right), ((x + k) % NX, left))[way]
        part = hid.at[shard, way * U:(way + 1) * U]
        return pltpu.make_async_remote_copy(
            src_ref=part, dst_ref=part, send_sem=sem_hs.at[k, way], recv_sem=sem_hr.at[k, way],
            device_id=(me, z * NX + to), device_id_type=MESH,
        )

    for way in range(2):
        hring(0, way).start()

    prow, pcol = iota((HALF * PAD, ROWS), 0), iota((HALF * PAD, ROWS), 1)
    spread = jnp.logical_and(pcol == (prow >> 4) * CAP + (prow & 15), (prow & 15) < CAP)
    spread = jnp.where(spread, 1.0, 0.0).astype(BF16)

    def project(k):
        for way in range(2):
            shard = ((x - k + NX) % NX, (x + k) % NX)[way]
            rows = nt(spread, hid[shard, way * U:(way + 1) * U, :]).astype(BF16)
            for f in range(2):
                out_acc[f] += nn(rows, wdn[f, units(shard, way), :])

    def relay_wait(k, _):
        for f in range(2):
            relay(k, f).wait_recv()
        return 0

    lax.fori_loop(0, NX, relay_wait, 0)
    out_acc[...] = jnp.zeros_like(out_acc)
    project(0)

    def hidden_step(k, _):
        for way in range(2):
            hring(k - 1, way).wait_recv()

            @pl.when(k < NX - 1)
            def _():
                hring(k, way).start()
        project(k)
        return 0

    lax.fori_loop(1, NX, hidden_step, 0)
    ret_src[...] = out_acc[...].astype(BF16).reshape(2, HALF, PAD, F)

    def give_back(i, _):
        for f in range(2):
            here = jnp.logical_and(2 * i + z == me, f == z)

            @pl.when(here)
            def _():
                pltpu.make_async_copy(ret_src.at[f, i], ret_buf.at[me], sem_ret.at[1]).start()

            @pl.when(jnp.logical_not(here))
            def _():
                pltpu.make_async_remote_copy(
                    src_ref=ret_src.at[f, i], dst_ref=ret_buf.at[me],
                    send_sem=sem_ret.at[0], recv_sem=sem_ret.at[1],
                    device_id=(2 * i + z, f * NX + x), device_id_type=MESH,
                ).start()
        return 0

    lax.fori_loop(0, HALF, give_back, 0)

    for sem, buf in ((sem_disp.at[0], send_buf), (sem_ret.at[0], ret_buf)):
        @pl.when(own)
        def _():
            pltpu.make_async_copy(buf.at[0:E - 1], buf.at[0:E - 1], sem).wait()

        @pl.when(jnp.logical_not(own))
        def _():
            pltpu.make_async_copy(buf, buf, sem).wait()
    for c in send_w1:
        c.wait_send()

    def sent(k, _):
        for f in range(2):
            relay(k, f).wait_send()

            @pl.when(k > 0)
            def _():
                down(k, f).wait_send()

            @pl.when(k < NX - 1)
            def _():
                for c in range(CHUNKS):
                    ring(k, c, f).wait_send()
                hring(k, f).wait_send()
        return 0

    lax.fori_loop(0, NX, sent, 0)

    pltpu.make_async_copy(ret_buf, ret_buf, sem_ret.at[1]).wait()
    back = ret_buf[...].reshape(E * PAD, F)
    out_ref[...] = (tn(comb[0], back) + tn(comb[1], back)).astype(BF16)


def solution(mesh):
    E, T = mesh.shape["expert"], mesh.shape["tensor"]
    NX = T // 2

    def local(tokens, expert_ids, gate_weights, w_gate, w_up, w_down):
        tok, F = tokens.shape
        U = w_gate.shape[2]
        HALF = E // 2
        ROWS = HALF * CAP
        vmem = pl.BlockSpec(memory_space=pltpu.VMEM)
        hbm = pl.BlockSpec(memory_space=pl.ANY)
        dma = pltpu.SemaphoreType.DMA
        return pl.pallas_call(
            functools.partial(kernel, E, NX),
            out_shape=jax.ShapeDtypeStruct((tok, F), BF16),
            in_specs=[vmem, vmem, vmem, hbm, hbm, hbm],
            out_specs=vmem,
            scratch_shapes=[
                pltpu.VMEM((E, PAD, F), BF16),
                pltpu.VMEM((2, HALF, PAD, F), BF16),
                pltpu.VMEM((NX, ROWS, F), BF16),
                pltpu.VMEM((NX, ROWS, F), BF16),
                pltpu.VMEM((2, 2 * U, T * F), BF16),
                pltpu.VMEM((2, 2 * U, ROWS), F32),
                pltpu.VMEM((NX, 2 * U, ROWS), BF16),
                pltpu.VMEM((2, T * U, F), BF16),
                pltpu.VMEM((2, HALF * PAD, F), F32),
                pltpu.VMEM((2, HALF, PAD, F), BF16),
                pltpu.VMEM((E, PAD, F), BF16),
                pltpu.VMEM((2, E * PAD, tok), BF16),
                dma((4,)),
                dma((2,)),
                dma((2, 2)),
                dma((NX, 2)),
                dma((NX, 2)),
                dma((2, NX, 2)),
                dma((NX, CHUNKS, 2)),
                dma((NX, CHUNKS, 2)),
                dma((NX, 2)),
                dma((NX, 2)),
                dma((2,)),
            ],
            compiler_params=pltpu.CompilerParams(
                collective_id=0, has_side_effects=True, vmem_limit_bytes=48 * 2**20
            ),
        )(
            tokens,
            expert_ids.T,
            gate_weights.T,
            w_gate[0].T,
            w_up[0].T,
            w_down[0],
        )

    placed = (
        P("expert", "tensor"),
        P("expert", None),
        P("expert", None),
        P("expert", None, "tensor"),
        P("expert", None, "tensor"),
        P("expert", "tensor", None),
    )
    return jax.shard_map(
        local, mesh=mesh, in_specs=placed, out_specs=P("expert", "tensor"), check_vma=False
    )
```

time: 277 us -> 130 us (0.47)
  Pallas kernels: 0 us -> 124 us
  waiting for transfers between devices: 122 us -> 0 us
  blocking collectives: 93.3 us -> 0 us
  starting transfers between devices: 25.4 us -> 0 us
  between operations: 13.5 us -> 0.02 us
  matrix products: 11.1 us -> 0 us
  other arithmetic: 6.02 us -> 0 us
    pallas_call x0 -> x1, Pallas kernels: none -> 124 us  [local(): pl.pallas_call(functools.partial(kernel, E, NX), out_shape=jax.ShapeDtype...]
    all_gather x1 -> x0, waiting for transfers between devices: 103 us -> none  [local(): lax.all_gather(arrived, 'tensor', axis=1, tiled=True)]
    all_to_all x2 -> x0, blocking collectives: 93.3 us -> none  [the longest x1 50.4 us: copy_for_each(): return lax.all_to_all(copies, axis, split_axis=0, concat_axis=0, tiled=True)]
    all_to_all x2 -> x0, starting transfers between devices: 25.4 us -> none  [the longest x1 17 us: local(): lax.all_to_all(expert_out, 'expert', split_axis=1, concat_axis=1, tiled=T...]
    all_to_all x2 -> x0, waiting for transfers between devices: 19.6 us -> none  [the longest x1 19.6 us: local(): lax.all_to_all(expert_out, 'expert', split_axis=1, concat_axis=1, tiled=T...]
    dot_general x4 -> x0, matrix products: 11.1 us -> none  [the longest x1 5 us: local(): jnp.dot(lax.all_gather(arrived, 'tensor', axis=1, tiled=True), weight_blo...]
    unnamed x12 -> x13, local copies, waits for them, and re-layouts: 1.03 us -> 5.47 us
    reduce_sum x2 -> x0, other arithmetic: 3.98 us -> none  [the longest x1 3.85 us: local(): summed = jnp.sum(rounded.astype(jnp.float32), axis=0)]
  transfers between devices with their start and end apart: 3 -> 0, of which waited for: 2 -> 0; matrix products, arithmetic and copies ran while one was open for 2% -> 0% of each run, Pallas kernels for 0% -> 0%
where the time goes in v1:
time: 130 us; the launch traced here: 129 us
  Pallas kernels  124 us (95%)
  local copies, waits for them, and re-layouts  5.47 us (4%)
    pallas_call x1, Pallas kernels, local(): pl.pallas_call(functools.partial(kernel, E, NX), out_shape=jax.ShapeDtype...  124 us
    unnamed x13, local copies, waits for them, and re-layouts  5.47 us

profile of v1, /device:TPU:1, one launch (start us, length us, event | category | flops | bytes accessed | tf_op | source)
XLA Modules:
  0.0 129.4 jit_solution(11582067358342528486)
XLA Ops:
  0.0 0.0 copy-start.5
  0.0 0.0 copy-start.4
  0.0 0.7 copy-done.5
  0.7 0.0 copy-done.4
  0.7 0.0 copy-start
  0.7 1.1 copy-done
  1.8 0.0 copy-start.1
  1.8 1.1 copy-done.1
  3.0 0.0 copy-start.2
  3.0 1.1 copy-done.2
  4.1 0.0 copy-start.3
  4.1 0.8 copy-done.3
  4.9 123.9 %shard_map.64 = bf16[64,256]{1,0:T(8,128)(2,1)S(1)} custom-call(bf16[64,256]{1,0:T(8,128)(2,1)S(1)} %copy-done.3, s32[8,64]{1,0:T(8,128)S(1)} %bitcast.12, f32[8,64]{1,0:T(8,128)S(1)} %bitcast.13, bf16[96,4096]{1,0:T(8,128)(2,1)S(1)} %bitcast.9, bf16[96,4096]{1,0:T(8,128)(2,1)S(1)} %bitcast.10, bf16[96,4096]{1,0:T(8,128)(2,1)S(1)} %bitcast.11), custom_call_target="tpu_custom_call" | custom-call | tf_op jit(solution)/shard_map/pallas_call | solution.py:332
  128.8 0.6 copy.8
Async XLA Ops:
  0.0 0.7 copy-start.5
  0.0 0.7 copy-start.4
  0.7 1.1 copy-start
  1.8 1.1 copy-start.1
  3.0 1.1 copy-start.2
  4.1 0.8 copy-start.3

commit v2 on v0

v2 whole, which is shorter than its diff:
```python
import functools

import jax
import jax.numpy as jnp
from jax import lax
from jax.experimental import pallas as pl
from jax.experimental.pallas import tpu as pltpu
from jax.sharding import PartitionSpec as P

MESH = pl.DeviceIdType.MESH
BF16, F32, I32 = jnp.bfloat16, jnp.float32, jnp.int32
CAP = 12
PAD = 16
LAG = 2


def nt(a, b):
    return lax.dot_general(a, b, (((1,), (1,)), ((), ())), preferred_element_type=F32)


def nn(a, b):
    return jnp.dot(a, b, preferred_element_type=F32)


def tn(a, b):
    return lax.dot_general(a, b, (((0,), (0,)), ((), ())), preferred_element_type=F32)


def iota(shape, dim):
    return lax.broadcasted_iota(I32, shape, dim)


def loop(low, high, body):
    def step(k, carry):
        body(k)
        return carry

    lax.fori_loop(low, high, step, 0)


def kernel(
    E, NX,
    tok_ref, ids_ref, gw_ref, wg_ref, wu_ref, wd_ref, out_ref,
    send_buf, recv_buf, xs, w1, acc, hid, wdn, wrel, out_acc, ret_src, ret_buf, comb,
    sem_ds, sem_dr, sem_w1s, sem_w1r, sem_wds, sem_wdr, sem_wfs, sem_wfr, sem_wl,
    sem_xs, sem_xr, sem_hs, sem_hr, sem_rs, sem_rr,
):
    HALF = E // 2
    HB = HALF // 2
    TOK, F = tok_ref.shape
    U = wg_ref.shape[0]
    ROWS = HALF * CAP
    RQ = ROWS // 2
    J = F // 2
    FAR = NX // 2
    me = lax.axis_index("expert")
    s = lax.axis_index("tensor")
    z, x = s // NX, s % NX
    pair, core = me // 2, me % 2
    right, left = (x + 1) % NX, (x + NX - 1) % NX
    other = 1 - z
    work = pair * 2 + z
    home = core == z
    place = (pair % 2) * HB + pair // 2
    across = (me, other * NX + x)
    sibling = (pair * 2 + 1 - core, s)

    def remote(src, dst, send, recv, to):
        return pltpu.make_async_remote_copy(
            src_ref=src, dst_ref=dst, send_sem=send, recv_sem=recv, device_id=to, device_id_type=MESH
        )

    def when(condition, body):
        pl.when(condition)(body)

    away = jnp.logical_not(home)

    barrier = pltpu.get_barrier_semaphore()

    def hello(to):
        pl.semaphore_signal(barrier, inc=1, device_id=to, device_id_type=MESH)

    hello(sibling)
    loop(1, NX, lambda d: hello((me, z * NX + (x + d) % NX)))

    def greet(i):
        for zz in range(2):
            when(
                jnp.logical_not(jnp.logical_and(i == pair, zz == z)),
                lambda: hello((2 * i + core, zz * NX + x)),
            )

    loop(0, HALF, greet)

    ids = ids_ref[...]
    expert = iota((E, TOK), 0)
    member = jnp.zeros((E, TOK), jnp.bool_)
    for k in range(ids.shape[0]):
        member = jnp.logical_or(member, ids[k:k + 1, :] == expert)
    before = (iota((TOK, TOK), 0) < iota((TOK, TOK), 1)).astype(BF16)
    rank = nn(member.astype(F32).astype(BF16), before).astype(I32)
    rank = jnp.where(member, rank, PAD)
    chosen = iota((E, PAD, TOK), 1) == rank[:, None, :]
    select = jnp.where(chosen, 1.0, 0.0).reshape(E * PAD, TOK).astype(BF16)
    send_buf[...] = nn(select, tok_ref[...]).astype(BF16).reshape(E, PAD, F)

    pl.semaphore_wait(barrier, 2 * HALF - 1 + NX)

    def cols(zz, xx):
        return pl.ds(pl.multiple_of(zz * (NX * F) + xx * F, F), F)

    def part(zz, j):
        return w1.at[zz, j * U:(j + 1) * U]

    def w1_own(j, to):
        return remote((wg_ref, wu_ref)[j], part(z, j), sem_w1s.at[0, j], sem_w1r.at[z, j], to)

    def w1_local(j):
        return pltpu.make_async_copy((wg_ref, wu_ref)[j], part(z, j), sem_w1r.at[z, j])

    def w1_pass(j):
        return remote(part(other, j), part(other, j), sem_w1s.at[1, j], sem_w1r.at[other, j], sibling)

    def w1_start():
        for j in range(2):
            when(away, lambda: w1_own(j, across).start())
        for j in range(2):
            when(home, lambda: w1_own(j, sibling).start())
            when(home, lambda: w1_local(j).start())

    def w1_arrived(zz):
        for j in range(2):
            pltpu.make_async_copy(part(zz, j), part(zz, j), sem_w1r.at[zz, j]).wait()

    def units(xx):
        return pl.ds(pl.multiple_of(xx * U, U), U)

    def down(d, f, buf):
        to = (x + d) % NX
        return remote(
            wd_ref.at[:, cols(f, to)], buf.at[f, units(x)], sem_wds.at[d, f], sem_wdr.at[d, f],
            (me, z * NX + to),
        )

    def down_local(f, buf):
        return pltpu.make_async_copy(wd_ref.at[:, cols(f, x)], buf.at[f, units(x)], sem_wl.at[f])

    def down_all(buf, act):
        loop(1, NX, lambda d: [act(down(d, f, buf)) for f in range(2)])

    def down_start(buf):
        for f in range(2):
            down_local(f, buf).start()
        down_all(buf, lambda c: c.start())

    def down_arrived(buf):
        for f in range(2):
            down_local(f, buf).wait()
        down_all(buf, lambda c: c.wait_recv())

    def wd_pass(src, zz, to):
        return remote(src, wdn.at[zz], sem_wfs.at[zz], sem_wfr.at[zz], to)


    def lanes(j):
        return pl.ds(j * J, J)

    def dispatch(j):
        def one(e):
            here = e == work
            src, dst = send_buf.at[e, :, lanes(j)], recv_buf.at[z, place, :, lanes(j)]
            when(here, lambda: pltpu.make_async_copy(src, dst, sem_dr.at[j]).start())
            to = ((e // 2) * 2 + core, (e % 2) * NX + x)
            when(
                jnp.logical_not(here),
                lambda: remote(src, dst, sem_ds.at[j], sem_dr.at[j], to).start(),
            )

        loop(0, E, one)


    when(home, lambda: down_start(wdn.at[z]))
    when(away, lambda: down_start(wrel))
    dispatch(0)
    dispatch(1)
    w1_start()

    weight = jnp.zeros((E, TOK), F32)
    for k in range(ids.shape[0]):
        weight = weight + jnp.where(ids[k:k + 1, :] == expert, gw_ref[k:k + 1, :], 0.0)
    weights = jnp.where(chosen, weight[:, None, :], 0.0).reshape(E * PAD, TOK)
    high = weights.astype(BF16)
    comb[0] = high
    comb[1] = (weights - high.astype(F32)).astype(BF16)
    acc[...] = jnp.zeros_like(acc)
    out_acc[...] = jnp.zeros_like(out_acc)

    def shards(k):
        return [x] if k == 0 else [(x + k) % NX] if k == FAR else [(x - k + NX) % NX, (x + k) % NX]

    def ring(q, k, j, way):
        shard, to = (((x - k + NX) % NX, right), ((x + k) % NX, left))[way]
        halves = way if k == FAR - 1 else slice(None)
        piece = xs.at[halves, shard, pl.ds(q * RQ, RQ), lanes(j)]
        return remote(piece, piece, sem_xs.at[q, k, j, way], sem_xr.at[q, k, j, way], (me, z * NX + to))

    def hring(q, k, way):
        shard, to = (((x - k + NX) % NX, right), ((x + k) % NX, left))[way]
        piece = hid.at[q, shard, way] if k == FAR - 1 else hid.at[q, shard]
        return remote(piece, piece, sem_hs.at[q, k, way], sem_hr.at[q, k, way], (me, z * NX + to))

    def ring_step(q, k):
        for j in range(2):
            for way in range(2):
                ring(q, k - 1, j, way).wait_recv()
                if k < FAR:
                    ring(q, k, j, way).start()

    def hring_step(q, k):
        for way in range(2):
            hring(q, k - 1, way).wait_recv()
            if k < FAR:
                hring(q, k, way).start()

    def multiply(q, zz, shard):
        rows = pl.ds(q * RQ, RQ)
        acc[q, zz] += nt(w1[zz, :, cols(0, shard)], xs[0, shard, rows]) + nt(w1[zz, :, cols(1, shard)], xs[1, shard, rows])

    def multiply_step(q, zz, k):
        for shard in shards(k):
            multiply(q, zz, shard)

    L = 2 * RQ // 3
    sides = [
        jnp.where(iota((RQ, L), 0) == iota((RQ, L), 1) + (L - side * (RQ - L)), 1.0, 0.0)
        * jnp.where((iota((RQ, L), 1) >= RQ - L) == (side == 1), 1.0, 0.0)
        for side in range(2)
    ]
    sides = [a.astype(BF16) for a in sides]
    spread = iota((RQ, HB * PAD), 0) == (iota((RQ, HB * PAD), 1) >> 4) * CAP + (iota((RQ, HB * PAD), 1) & 15)
    spread = jnp.logical_and(spread, (iota((RQ, HB * PAD), 1) & 15) < CAP)
    spread = jnp.where(spread, 1.0, 0.0).astype(BF16)

    def activate(q):
        for zz in range(2):
            g, u = acc[q, zz, 0:U, :], acc[q, zz, U:2 * U, :]
            h = (g / (1.0 + jnp.exp(-g)) * u).astype(BF16)
            hid[q, x, zz, 0:U, :] = h[:, 0:L]
            hid[q, x, zz, U:U + U // 2, :] = (nn(h[0:U // 2], sides[0]) + nn(h[U // 2:U], sides[1])).astype(BF16)
        for way in range(2):
            hring(q, 0, way).start()

    def project(q, shard):
        for way in range(2):
            low, high = hid[q, shard, way, 0:U, :], hid[q, shard, way, U:U + U // 2, :]
            for f in range(2):
                down_rows = wdn[way, f, units(shard), :]
                out_acc[q, f, 0:L, :] += tn(low, down_rows)
                first, last = tn(high, down_rows[0:U // 2]), tn(high, down_rows[U // 2:U])
                out_acc[q, f, L:RQ, :] += first[0:RQ - L] + last[RQ - L:]

    def give_back(q):
        for f in range(2):
            ret_src[q, f] = tn(spread, out_acc[q, f].astype(BF16)).astype(BF16).reshape(HB, PAD, F)

        def one(t):
            i = 2 * t + q
            for f in range(2):
                here = jnp.logical_and(i == pair, f == z)
                src, dst = ret_src.at[q, f, t], ret_buf.at[work]
                when(here, lambda: pltpu.make_async_copy(src, dst, sem_rr.at[0]).start())
                when(
                    jnp.logical_not(here),
                    lambda: remote(src, dst, sem_rs.at[0], sem_rr.at[0], (2 * i + core, f * NX + x)).start(),
                )

        loop(0, HB, one)

    row, col = iota((ROWS, HALF * PAD), 0), iota((ROWS, HALF * PAD), 1)
    pack = jnp.logical_and(row == (col >> 4) * CAP + (col & 15), (col & 15) < CAP)
    pack = jnp.where(pack, 1.0, 0.0).astype(BF16)

    def arrived(sem, j):
        pltpu.make_async_copy(send_buf.at[:, :, lanes(j)], send_buf.at[:, :, lanes(j)], sem).wait()

    for j in range(2):
        arrived(sem_dr.at[j], j)
        for way in range(2):
            rows = recv_buf[way, :, :, j * J:(j + 1) * J].reshape(HALF * PAD, J)
            xs[way, x, :, j * J:(j + 1) * J] = nn(pack, rows).astype(BF16)
        for way in range(2):
            ring(0, 0, j, way).start()
    for j in range(2):
        for way in range(2):
            ring(1, 0, j, way).start()
    w1_arrived(z)
    multiply_step(0, z, 0)
    for n in range(1, FAR + 1):
        ring_step(0, n)
        if n > LAG:
            ring_step(1, n - LAG)
        multiply_step(0, z, n)
        if n >= LAG:
            multiply_step(1, z, n - LAG)

    w1_arrived(other)

    def pass_w():
        for j in range(2):
            w1_pass(j).start()
        down_arrived(wdn.at[z])
        wd_pass(wdn.at[z], z, sibling).start()

    def cross_w():
        down_arrived(wrel)
        wd_pass(wrel, z, across).start()

    when(home, pass_w)
    when(away, cross_w)
    loop(0, NX, lambda k: multiply(0, other, k))
    activate(0)

    def wd_arrived(zz):
        pltpu.make_async_copy(wdn.at[zz], wdn.at[zz], sem_wfr.at[zz]).wait()

    for m in range(1, LAG + 1):
        ring_step(1, FAR - LAG + m)
        hring_step(0, m)
        multiply_step(1, z, FAR - LAG + m)
    loop(0, NX, lambda k: multiply(1, other, k))
    activate(1)

    def wd_home():
        wd_arrived(other)
        wd_pass(wdn.at[other], other, sibling).start()

    def wd_away():
        wd_arrived(z)
        wd_arrived(other)

    when(home, wd_home)
    when(away, wd_away)

    def project_steps(q, low, high):
        for k in range(low, high + 1):
            for shard in shards(k):
                project(q, shard)

    project(0, x)
    loop(1, LAG + 1, lambda k: [project(0, (x - k + NX) % NX), project(0, (x + k) % NX)])
    for m in range(1, FAR - LAG + 1):
        hring_step(0, LAG + m)
        hring_step(1, m)
        project_steps(0, LAG + m, LAG + m)
    give_back(0)
    project(1, x)
    loop(1, FAR - LAG + 1, lambda k: [project(1, (x - k + NX) % NX), project(1, (x + k) % NX)])
    for m in range(1, LAG + 1):
        hring_step(1, FAR - LAG + m)
        project_steps(1, FAR - LAG + m, FAR - LAG + m)
    give_back(1)

    for j in range(2):
        sent = send_buf.at[0:E - 1, :, lanes(j)]
        pltpu.make_async_copy(sent, sent, sem_ds.at[j]).wait()
    for j in range(2):
        w1_own(j, sibling).wait_send()
        when(home, lambda: w1_pass(j).wait_send())
    wd_pass(wdn.at[z], z, sibling).wait_send()
    when(home, lambda: wd_pass(wdn.at[other], other, sibling).wait_send())
    down_all(wrel, lambda c: c.wait_send())

    for q in range(2):
        for k in range(FAR):
            for way in range(2):
                hring(q, k, way).wait_send()
                for j in range(2):
                    ring(q, k, j, way).wait_send()

    sent = ret_buf.at[0:E - 1]
    pltpu.make_async_copy(sent, sent, sem_rs.at[0]).wait()

    pltpu.make_async_copy(ret_buf, ret_buf, sem_rr.at[0]).wait()
    back = ret_buf[...].reshape(E * PAD, F)
    out_ref[...] = (tn(comb[0], back) + tn(comb[1], back)).astype(BF16)


def solution(mesh):
    E, T = mesh.shape["expert"], mesh.shape["tensor"]
    NX = T // 2

    def local(tokens, expert_ids, gate_weights, w_gate, w_up, w_down):
        tok, F = tokens.shape
        U = w_gate.shape[2]
        HALF = E // 2
        HB = HALF // 2
        ROWS = HALF * CAP
        RQ = ROWS // 2
        vmem = pl.BlockSpec(memory_space=pltpu.VMEM)
        hbm = pl.BlockSpec(memory_space=pl.ANY)
        dma = pltpu.SemaphoreType.DMA
        return pl.pallas_call(
            functools.partial(kernel, E, NX),
            out_shape=jax.ShapeDtypeStruct((tok, F), BF16),
            in_specs=[vmem, vmem, vmem, hbm, hbm, hbm],
            out_specs=vmem,
            scratch_shapes=[
                pltpu.VMEM((E, PAD, F), BF16),
                pltpu.VMEM((2, HALF, PAD, F), BF16),
                pltpu.VMEM((2, NX, ROWS, F), BF16),
                pltpu.VMEM((2, 2 * U, T * F), BF16),
                pltpu.VMEM((2, 2, 2 * U, RQ), F32),
                pltpu.VMEM((2, NX, 2, U + U // 2, 2 * RQ // 3), BF16),
                pltpu.VMEM((2, 2, NX * U, F), BF16),
                pltpu.VMEM((2, NX * U, F), BF16),
                pltpu.VMEM((2, 2, RQ, F), F32),
                pltpu.VMEM((2, 2, HB, PAD, F), BF16),
                pltpu.VMEM((E, PAD, F), BF16),
                pltpu.VMEM((2, E * PAD, tok), BF16),
                dma((2,)),
                dma((2,)),
                dma((2, 2)),
                dma((2, 2)),
                dma((NX, 2)),
                dma((NX, 2)),
                dma((2,)),
                dma((2,)),
                dma((2,)),
                dma((2, NX // 2, 2, 2)),
                dma((2, NX // 2, 2, 2)),
                dma((2, NX // 2, 2)),
                dma((2, NX // 2, 2)),
                dma((1,)),
                dma((1,)),
            ],
            compiler_params=pltpu.CompilerParams(
                collective_id=0, has_side_effects=True, vmem_limit_bytes=60 * 2**20
            ),
        )(
            tokens,
            expert_ids.T,
            gate_weights.T,
            w_gate[0].T,
            w_up[0].T,
            w_down[0],
        )

    placed = (
        P("expert", "tensor"),
        P("expert", None),
        P("expert", None),
        P("expert", None, "tensor"),
        P("expert", None, "tensor"),
        P("expert", "tensor", None),
    )
    return jax.shard_map(
        local, mesh=mesh, in_specs=placed, out_specs=P("expert", "tensor"), check_vma=False
    )
```

time: 277 us -> 108 us (0.39)
  the two profiles are of different devices: /device:TPU:1 before, /device:TPU:30 now
where the time goes in v2:
time: 108 us
  Pallas kernels  106 us (98%)
  local copies, waits for them, and re-layouts  1.38 us (1%)
    pallas_call x1, Pallas kernels, local(): pl.pallas_call(functools.partial(kernel, E, NX), out_shape=jax.ShapeDtype...  106 us

profile of v2, /device:TPU:30, one launch (start us, length us, event | category | flops | bytes accessed | tf_op | source)
XLA Modules:
  0.0 107.6 jit_solution(17128466565924726355)
XLA Ops:
  0.0 106.3 %shard_map.64 = bf16[64,256]{1,0:T(8,128)(2,1)} custom-call(bf16[64,256]{1,0:T(8,128)(2,1)} %tok_ref.1, s32[8,64]{1,0:T(8,128)} %bitcast.12, f32[8,64]{1,0:T(8,128)} %bitcast.13, bf16[96,4096]{1,0:T(8,128)(2,1)} %bitcast.9, bf16[96,4096]{1,0:T(8,128)(2,1)} %bitcast.10, bf16[96,4096]{1,0:T(8,128)(2,1)} %bitcast.11), custom_call_target="tpu_custom_call" | custom-call | tf_op jit(solution)/shard_map/pallas_call | solution.py:402
  106.3 1.4 %copy.8 = bf16[64,256]{1,0:T(8,128)(2,1)} copy(bf16[64,256]{1,0:T(8,128)(2,1)} %shard_map.64) | data formatting | bytes 65536

commit v3 on v2

--- a/solution.py
+++ b/solution.py
@@ -190,8 +190,10 @@
         weight = weight + jnp.where(ids[k:k + 1, :] == expert, gw_ref[k:k + 1, :], 0.0)
     weights = jnp.where(chosen, weight[:, None, :], 0.0).reshape(E * PAD, TOK)
     high = weights.astype(BF16)
-    comb[0] = high
-    comb[1] = (weights - high.astype(F32)).astype(BF16)
+    low = (weights - high.astype(F32)).astype(BF16)
+    eye = jnp.where(iota((TOK, TOK), 0) == iota((TOK, TOK), 1), 1.0, 0.0).astype(BF16)
+    comb[0:TOK, :] = nt(eye, high).astype(BF16)
+    comb[TOK:2 * TOK, :] = nt(eye, low).astype(BF16)
     acc[...] = jnp.zeros_like(acc)
     out_acc[...] = jnp.zeros_like(out_acc)
 
@@ -293,18 +295,6 @@
     for j in range(2):
         for way in range(2):
             ring(1, 0, j, way).start()
-    w1_arrived(z)
-    multiply_step(0, z, 0)
-    for n in range(1, FAR + 1):
-        ring_step(0, n)
-        if n > LAG:
-            ring_step(1, n - LAG)
-        multiply_step(0, z, n)
-        if n >= LAG:
-            multiply_step(1, z, n - LAG)
-
-    w1_arrived(other)
-
     def pass_w():
         for j in range(2):
             w1_pass(j).start()
@@ -315,19 +305,34 @@
         down_arrived(wrel)
         wd_pass(wrel, z, across).start()
 
-    when(home, pass_w)
-    when(away, cross_w)
-    loop(0, NX, lambda k: multiply(0, other, k))
+    w1_arrived(z)
+    multiply_step(0, z, 0)
+    for n in range(1, FAR + 1):
+        if n == FAR:
+            w1_arrived(other)
+            when(home, pass_w)
+            when(away, cross_w)
+            loop(0, NX - 1, lambda k: multiply(0, other, (x + FAR + 1 + k) % NX))
+        ring_step(0, n)
+        if n > LAG:
+            ring_step(1, n - LAG)
+        multiply_step(0, z, n)
+        if n < FAR and n >= LAG:
+            multiply_step(1, z, n - LAG)
+    multiply_step(0, other, FAR)
     activate(0)
+    multiply_step(1, z, FAR - LAG)
 
     def wd_arrived(zz):
         pltpu.make_async_copy(wdn.at[zz], wdn.at[zz], sem_wfr.at[zz]).wait()
 
     for m in range(1, LAG + 1):
+        if m == LAG:
+            loop(0, NX - 1, lambda k: multiply(1, other, (x + FAR + 1 + k) % NX))
         ring_step(1, FAR - LAG + m)
         hring_step(0, m)
         multiply_step(1, z, FAR - LAG + m)
-    loop(0, NX, lambda k: multiply(1, other, k))
+    multiply_step(1, other, FAR)
     activate(1)
 
     def wd_home():
@@ -382,7 +387,8 @@
 
     pltpu.make_async_copy(ret_buf, ret_buf, sem_rr.at[0]).wait()
     back = ret_buf[...].reshape(E * PAD, F)
-    out_ref[...] = (tn(comb[0], back) + tn(comb[1], back)).astype(BF16)
+    mixed = nn(comb[...], back)
+    out_ref[...] = (mixed[0:TOK] + mixed[TOK:2 * TOK]).astype(BF16)
 
 
 def solution(mesh):
@@ -416,7 +422,7 @@
                 pltpu.VMEM((2, 2, RQ, F), F32),
                 pltpu.VMEM((2, 2, HB, PAD, F), BF16),
                 pltpu.VMEM((E, PAD, F), BF16),
-                pltpu.VMEM((2, E * PAD, tok), BF16),
+                pltpu.VMEM((2 * tok, E * PAD), BF16),
                 dma((2,)),
                 dma((2,)),
                 dma((2, 2)),

time: 108 us -> 104 us (0.963)
  the two profiles are of different devices: /device:TPU:30 before, /device:TPU:1 now
where the time goes in v3:
time: 104 us; the launch traced here: 102 us
  Pallas kernels  101 us (97%)
  local copies, waits for them, and re-layouts  1.38 us (1%)
    pallas_call x1, Pallas kernels, local(): pl.pallas_call(functools.partial(kernel, E, NX), out_shape=jax.ShapeDtype...  101 us

profile of v3, /device:TPU:1, one launch (start us, length us, event | category | flops | bytes accessed | tf_op | source)
XLA Modules:
  0.0 102.0 jit_solution(16986619842151632434)
XLA Ops:
  0.0 100.6 %shard_map.64 = bf16[64,256]{1,0:T(8,128)(2,1)} custom-call(bf16[64,256]{1,0:T(8,128)(2,1)} %tok_ref.1, s32[8,64]{1,0:T(8,128)} %bitcast.12, f32[8,64]{1,0:T(8,128)} %bitcast.13, bf16[96,4096]{1,0:T(8,128)(2,1)} %bitcast.9, bf16[96,4096]{1,0:T(8,128)(2,1)} %bitcast.10, bf16[96,4096]{1,0:T(8,128)(2,1)} %bitcast.11), custom_call_target="tpu_custom_call" | custom-call | tf_op jit(solution)/shard_map/pallas_call | solution.py:408
  100.6 1.4 %copy.8 = bf16[64,256]{1,0:T(8,128)(2,1)} copy(bf16[64,256]{1,0:T(8,128)(2,1)} %shard_map.64) | data formatting | bytes 65536
